TPU v7x, 256 devices: a whole 4x4x8 slice. The times are simulated.
256 devices in a mesh: mpo: 4 (over y), sector: 64 (over z, x, core).
Axes of the slice: x: 4, y: 4, z: 8, core: 2. Of those that a mesh axis runs over, the one named last changes fastest.
Arguments:
- wavefunction: bfloat16 [8192, 64, 128], P('sector'), may hold values from -6 to 6
- left_env: bfloat16 [8, 8192, 128], P('mpo', 'sector'), may hold values from -4 to 4
- right_env: bfloat16 [8, 8192, 128], P('mpo', 'sector'), may hold values from -2 to 2
- term_live: int32 [8, 64], P('mpo', 'sector'), may hold values 0 or 1
- block_live: int32 [64, 64], P('sector'), may hold values from 0 to 1, as said below
- sector_dims: int32 [64], replicated, may hold values from 96 to 128, as said below
Outputs:
- residual: bfloat16 [8192, 64, 128], P('sector')
- second_image: bfloat16 [8192, 64, 128], P('sector')
Inputs may be any that keep to these rules, and one draw needn't show every extreme that they name: `block_live`: every diagonal block (a, a) is allowed. `sector_dims`: some sector has all 128 rows used.
All inputs are finite; a program needn't handle non-finite values. No bound on the sum of `term_live` on one device may be relied on, other than what follows from the above.
Results may differ from a plain program's by a relative error of at most 0.025.
Values may be sent and summed in bfloat16 or wider, within the bound.
A program may use at most 64 MiB of HBM per device.

v0:
```python
import jax
import jax.numpy as jnp
from jax import lax
from jax.sharding import PartitionSpec as P


def extents(sector_dims, own_sector, tile_size):
    positions = lax.broadcasted_iota(jnp.int32, (tile_size,), 0)
    sectors = lax.broadcasted_iota(jnp.int32, sector_dims.shape, 0)
    own_dim = jnp.sum(jnp.where(sectors == own_sector, sector_dims, 0))
    return (positions < own_dim, positions[None, :] < sector_dims[:, None])


def left_half(matrix, vector):
    return jnp.einsum("ik,kbj->ibj", matrix, vector, preferred_element_type=jnp.float32).astype(
        jnp.bfloat16
    )


def empty_half(matrix, vector):
    return jnp.zeros(vector.shape, jnp.bfloat16)


def rayleigh_residual(state, first, site_axis_sum):
    state_wide = state.astype(jnp.float32)
    first_wide = first.astype(jnp.float32)
    norm_total, correlation = site_axis_sum(
        (jnp.sum(state_wide * state_wide), jnp.sum(state_wide * first_wide))
    )
    return (first_wide - correlation / norm_total * state_wide).astype(jnp.bfloat16)


def body(wavefunction, left_env, right_env, term_live, block_live, sector_dims):
    tile_size = wavefunction.shape[0]
    own_sector = lax.axis_index("sector")
    inside_own, inside_all = extents(sector_dims, own_sector, tile_size)
    row_mask = (
        (block_live[0] > 0)[None, :, None] & inside_own[:, None, None] & inside_all[None, :, :]
    )
    state = jnp.where(row_mask, wavefunction, jnp.zeros_like(wavefunction))

    def to_rows(summed):
        total = lax.psum(summed.astype(jnp.bfloat16), "mpo")
        return lax.all_to_all(total, "sector", split_axis=1, concat_axis=1, tiled=True)

    def right_half(piece):
        return jnp.einsum("tiak,tkj->iaj", piece, right_env, preferred_element_type=jnp.float32)

    def apply_rows(vector):
        contracted = []
        for term_index in range(left_env.shape[0]):
            contracted.append(
                lax.cond(
                    term_live[term_index, 0] > 0,
                    left_half,
                    empty_half,
                    left_env[term_index],
                    vector,
                )
            )
        stacked = jnp.stack(contracted)
        summed = right_half(
            lax.all_to_all(stacked, "sector", split_axis=2, concat_axis=2, tiled=True)
        )
        image = to_rows(summed)
        return jnp.where(row_mask, image, jnp.zeros_like(image))

    def row_sums(values):
        return lax.psum(values, "sector")

    first = apply_rows(state)
    residual = rayleigh_residual(state, first, row_sums)
    second_image = apply_rows(residual)
    return (residual, second_image)


def solution(mesh):
    return jax.shard_map(
        body,
        mesh=mesh,
        in_specs=(
            P("sector", None, None),
            P("mpo", "sector", None),
            P("mpo", "sector", None),
            P("mpo", "sector"),
            P("sector", None),
            P(),
        ),
        out_specs=(P("sector", None, None), P("sector", None, None)),
        check_vma=False,
    )
```

profile of v0, /device:TPU:1, one launch (start us, length us, event | category | flops | bytes accessed | tf_op | source)
XLA Modules:
  0.0 638.1 jit_solution(825621949123976493)
XLA Ops:
  7.2 0.0 copy-start
  7.2 0.0 all-reduce.4.cloned.1.call-start
  7.2 0.7 iota_compare_fusion
  8.0 1.3 fusion.9
  9.3 0.6 iota_compare_fusion.1
  9.9 0.7 compare_bitcast_fusion
  10.6 1.3 fusion.10
  13.2 0.8 slice_bitcast_fusion.1
  14.0 0.1 broadcast_and_fusion
  14.1 3.2 and_select_fusion.2
  17.3 2.0 conditional.4
  17.3 2.0 convert_bitcast_fusion
  19.3 2.0 conditional.5
  19.3 2.0 convert_bitcast_fusion.1
  21.3 2.6 pad_maximum_fusion
  24.0 107.2 %all_to_all.20 = bf16[2,128,64,128]{3,1,0,2:T(8,128)(2,1)S(1)} all-to-all(bf16[2,128,64,128]{3,1,0,2:T(8,128)(2,1)S(1)} %pad_maximum_fusion), channel_id=1, replica_groups=mesh['mpo'=4,'sector'=64] {'sector'}, dimensions={2} | all-to-all | bytes 8388608 | tf_op jit(solution)/shard_map/all_to_all | solution.py:63
  131.2 0.0 copy-done
  131.2 2.6 bitcast_convert_fusion.1
  133.8 0.0 all-reduce.4.cloned.1.call-update
  133.8 0.0 copy-start.1
  133.8 61.8 %all-reduce.4.cloned.1.call-done = bf16[128,64,128]{2,0,1:T(8,128)(2,1)} async-done(((bf16[128,64,128]{2,0,1:T(8,128)(2,1)}), bf16[128,64,128]{2,0,1:T(8,128)(2,1)}) %all-reduce.4.cloned.1.call-update) | async-done | bytes 2097168 | tf_op jit(solution)/shard_map/psum | solution.py:43
  195.6 10.8 %all-to-all-start.1 = ((bf16[128,64,128]{2,0,1:T(8,128)(2,1)}), bf16[128,64,128]{2,0,1:T(8,128)(2,1)}, u32[]{:S(2)}, u32[]{:S(2)}) async-start(bf16[128,64,128]{2,0,1:T(8,128)(2,1)} %all-reduce.4.cloned.1.call-done), calls=%async_computation.1 | async-start | bytes 4194304 | tf_op jit(solution)/shard_map/all_to_all | solution.py:44
  206.5 0.0 all-reduce.6.cloned.1.call-start
  206.5 49.5 %all-to-all-done.1 = bf16[128,64,128]{2,0,1:T(8,128)(2,1)} async-done(((bf16[128,64,128]{2,0,1:T(8,128)(2,1)}), bf16[128,64,128]{2,0,1:T(8,128)(2,1)}, u32[]{:S(2)}, u32[]{:S(2)}) %all-to-all-start.1) | async-done | bytes 2097184 | tf_op jit(solution)/shard_map/all_to_all | solution.py:44
  256.1 0.0 copy-done.1
  256.1 6.8 %fusion.6 = (f32[]{:T(128)}, f32[]{:T(128)}) fusion(bf16[128,64,128]{2,0,1:T(8,128)(2,1)} %all-to-all-done.1, pred[64,128]{1,0:T(8,128)(4,1)S(1)} %iota_compare_fusion, pred[128,64]{0,1:T(8,128)(4,1)S(1)} %broadcast_and_fusion, bf16[128,64,128]{2,1,0:T(8,128)(2,1)S(1)} %copy-done.1), kind=kLoop, calls=%fused_computation.17 | loop fusion | flops 9437182 | bytes 4210696 | tf_op jit(solution)/shard_map/reduce_sum | solution.py:28
  262.8 126.2 %all-reduce = (f32[]{:T(128)}, f32[]{:T(128)}) all-reduce(f32[]{:T(128)} %get-tuple-element.45, f32[]{:T(128)} %get-tuple-element.44), channel_id=1, replica_groups=mesh['mpo'=4,'sector'=64] {'sector'}, use_global_device_ids=true, to_apply=%region_7.8 | all-reduce | flops 2 | bytes 16 | tf_op jit(solution)/shard_map/psum | solution.py:69
  390.3 3.9 fusion.4
  394.2 2.0 conditional.6
  394.2 2.0 convert_bitcast_fusion.2
  396.2 2.0 conditional.7
  396.2 2.0 convert_bitcast_fusion.3
  398.3 2.6 pad_maximum_fusion.1
  400.9 101.3 %all_to_all.21 = bf16[2,128,64,128]{3,1,0,2:T(8,128)(2,1)S(1)} all-to-all(bf16[2,128,64,128]{3,1,0,2:T(8,128)(2,1)S(1)} %pad_maximum_fusion.1), channel_id=1, replica_groups=mesh['mpo'=4,'sector'=64] {'sector'}, dimensions={2} | all-to-all | bytes 8388608 | tf_op jit(solution)/shard_map/all_to_all | solution.py:63
  502.2 2.6 bitcast_convert_fusion
  504.7 0.0 all-reduce.6.cloned.1.call-update
  504.8 60.2 %all-reduce.6.cloned.1.call-done = bf16[128,64,128]{2,0,1:T(8,128)(2,1)} async-done(((bf16[128,64,128]{2,0,1:T(8,128)(2,1)}), bf16[128,64,128]{2,0,1:T(8,128)(2,1)}) %all-reduce.6.cloned.1.call-update) | async-done | bytes 2097168 | tf_op jit(solution)/shard_map/psum | solution.py:43
  565.0 10.8 %all-to-all-start.3 = ((bf16[128,64,128]{2,0,1:T(8,128)(2,1)}), bf16[128,64,128]{2,0,1:T(8,128)(2,1)}, u32[]{:S(2)}, u32[]{:S(2)}) async-start(bf16[128,64,128]{2,0,1:T(8,128)(2,1)} %all-reduce.6.cloned.1.call-done), calls=%async_computation.3 | async-start | bytes 4194304 | tf_op jit(solution)/shard_map/all_to_all | solution.py:44
  575.8 2.7 copy.13
  578.5 46.9 %all-to-all-done.3 = bf16[128,64,128]{2,0,1:T(8,128)(2,1)} async-done(((bf16[128,64,128]{2,0,1:T(8,128)(2,1)}), bf16[128,64,128]{2,0,1:T(8,128)(2,1)}, u32[]{:S(2)}, u32[]{:S(2)}) %all-to-all-start.3) | async-done | bytes 2097184 | tf_op jit(solution)/shard_map/all_to_all | solution.py:44
  625.4 3.2 and_select_fusion
  628.6 2.7 copy.14
Async XLA Ops:
  7.2 124.0 %copy-start = (bf16[2,128,128]{2,1,0:T(8,128)(2,1)S(1)}, bf16[2,128,128]{2,1,0:T(8,128)(2,1)}, u32[]{:S(2)}) copy-start(bf16[2,128,128]{2,1,0:T(8,128)(2,1)} %param.16) | copy-start | bytes 196612
  7.2 188.4 %all-reduce.4.cloned.1.call-start = ((), (), s32[]{:S(2)}) async-start(), calls=%async_computation.4 | async-start | bytes 4194304 | tf_op jit(solution)/shard_map/psum | solution.py:43
  133.8 122.3 %copy-start.1 = (bf16[128,64,128]{2,1,0:T(8,128)(2,1)S(1)}, bf16[128,64,128]{2,1,0:T(8,128)(2,1)}, u32[]{:S(2)}) copy-start(bf16[128,64,128]{2,1,0:T(8,128)(2,1)} %param.14) | copy-start | bytes 6291460
  195.6 60.4 %all-to-all-start.1 = ((bf16[128,64,128]{2,0,1:T(8,128)(2,1)}), bf16[128,64,128]{2,0,1:T(8,128)(2,1)}, u32[]{:S(2)}, u32[]{:S(2)}) async-start(bf16[128,64,128]{2,0,1:T(8,128)(2,1)} %all-reduce.4.cloned.1.call-done), calls=%async_computation.1 | async-start | bytes 4194304 | tf_op jit(solution)/shard_map/all_to_all | solution.py:44
  206.5 358.5 %all-reduce.6.cloned.1.call-start = ((), (), s32[]{:S(2)}) async-start(), calls=%async_computation.5 | async-start | bytes 4194304 | tf_op jit(solution)/shard_map/psum | solution.py:43
  565.0 60.4 %all-to-all-start.3 = ((bf16[128,64,128]{2,0,1:T(8,128)(2,1)}), bf16[128,64,128]{2,0,1:T(8,128)(2,1)}, u32[]{:S(2)}, u32[]{:S(2)}) async-start(bf16[128,64,128]{2,0,1:T(8,128)(2,1)} %all-reduce.6.cloned.1.call-done), calls=%async_computation.3 | async-start | bytes 4194304 | tf_op jit(solution)/shard_map/all_to_all | solution.py:44
Sparse Core Ops, SparseCore 0:
  133.9 61.6 all-reduce.3
  504.9 60.0 all-reduce.5
where the time goes:
time: 639 us; the launch traced here: 638 us
  blocking collectives  335 us (52%)
  waiting for transfers between devices  219 us (34%)
  other arithmetic  25.7 us (4%)
  starting transfers between devices  21.8 us (3%)
  between operations  16.8 us (3%)
  matrix products  13.2 us (2%)
  local copies, waits for them, and re-layouts  7.45 us (1%)
    all_to_all x2, blocking collectives, apply_rows(): lax.all_to_all(stacked, 'sector', split_axis=2, concat_axis=2, tiled=True)  208 us
    psum x1, blocking collectives, row_sums(): return lax.psum(values, 'sector')  126 us
    psum x2, waiting for transfers between devices, to_rows(): total = lax.psum(summed.astype(jnp.bfloat16), 'mpo')  122 us
    all_to_all x2, waiting for transfers between devices, to_rows(): lax.all_to_all(total, 'sector', split_axis=1, concat_axis=1, tiled=True)  96.5 us
    all_to_all x2, starting transfers between devices, to_rows(): lax.all_to_all(total, 'sector', split_axis=1, concat_axis=1, tiled=True)  21.7 us
  transfers between devices with their start and end apart: 4, of which 4 were waited for; matrix products, arithmetic and copies ran while one was open for 0% of the time, Pallas kernels for 0%

commit v1 on v0

v1 whole, which is shorter than its diff:
```python
import jax
import jax.numpy as jnp
from jax import lax
from jax.sharding import PartitionSpec as P

Z, X, C = 8, 4, 2


def body(wavefunction, left_env, right_env, term_live, block_live, sector_dims):
    n = wavefunction.shape[0]
    y_at = lax.axis_index("mpo")
    s_at = lax.axis_index("sector")
    places = jnp.arange(n, dtype=jnp.int32)
    inside = places[None, :] < sector_dims[:, None]
    own_rows = lax.dynamic_index_in_dim(inside, s_at, 0, keepdims=False)
    mask = (block_live[0] > 0)[None, :, None] & own_rows[:, None, None] & inside[None]
    state = jnp.where(mask, wavefunction, jnp.zeros_like(wavefunction))

    order = []
    for y in range(X):
        for z in range(Z):
            for x in range(X):
                for c in range(C):
                    order.append((y * Z * X * C + (z * X + x) * C + c, x * Z * X * C + (z * X + y) * C + c))
    right_here = lax.ppermute(right_env, ("mpo", "sector"), order)
    rights = lax.all_gather(right_here, "sector").reshape(Z, X, C, 2, n, n)
    rights = rights.transpose(0, 2, 1, 3, 4, 5).reshape(Z * C, 2 * X, n, n)
    lefts = jnp.where((term_live > 0)[:, :, None], left_env, jnp.zeros_like(left_env))
    lefts = lax.all_gather(lefts, "mpo", tiled=True)

    def own(full):
        part = lax.dynamic_index_in_dim(full.reshape(n, Z, X, C, n), y_at, 2, keepdims=False)
        return part.reshape(n, Z * C, n)

    mask_own = own(mask)

    def apply_own(vector):
        half = jnp.einsum("tik,kbj->btij", lefts, vector, preferred_element_type=jnp.float32).astype(jnp.bfloat16)
        image = jnp.einsum("btik,btkj->bij", half, rights, preferred_element_type=jnp.float32)
        image = image.transpose(1, 0, 2)
        return jnp.where(mask_own, image, 0.0).astype(jnp.bfloat16)

    def share(part):
        full = lax.all_gather(part, "mpo").reshape(X, n, Z, C, n)
        return full.transpose(1, 2, 0, 3, 4).reshape(n, Z * X * C, n)

    state_own = own(state)
    first_own = apply_own(state_own)
    wide, first_wide = state_own.astype(jnp.float32), first_own.astype(jnp.float32)
    sums = lax.psum(jnp.stack([jnp.sum(wide * first_wide), jnp.sum(wide * wide)]), ("mpo", "sector"))
    residual_own = (first_wide - sums[0] / sums[1] * wide).astype(jnp.bfloat16)
    second_own = apply_own(residual_own)
    return share(residual_own), share(second_own)


def solution(mesh):
    return jax.shard_map(
        body,
        mesh=mesh,
        in_specs=(
            P("sector", None, None),
            P("mpo", "sector", None),
            P("mpo", "sector", None),
            P("mpo", "sector"),
            P("sector", None),
            P(),
        ),
        out_specs=(P("sector", None, None), P("sector", None, None)),
        check_vma=False,
    )
```

time: 639 us -> 280 us (0.44)
  blocking collectives: 335 us -> 93.4 us
  waiting for transfers between devices: 219 us -> 128 us
  starting transfers between devices: 21.8 us -> 1.62 us
  other arithmetic: 25.7 us -> 9.53 us
  local copies, waits for them, and re-layouts: 7.45 us -> 20.8 us
    all_to_all x2 -> x0, blocking collectives: 208 us -> none  [apply_rows(): lax.all_to_all(stacked, 'sector', split_axis=2, concat_axis=2, tiled=True)]
    all_gather x0 -> x3, waiting for transfers between devices: none -> 127 us  [the longest x2 65.3 us: share(): full = lax.all_gather(part, 'mpo').reshape(X, n, Z, C, n)]
    psum x2 -> x0, waiting for transfers between devices: 122 us -> none  [to_rows(): total = lax.psum(summed.astype(jnp.bfloat16), 'mpo')]
    all_to_all x2 -> x0, waiting for transfers between devices: 96.5 us -> none  [to_rows(): lax.all_to_all(total, 'sector', split_axis=1, concat_axis=1, tiled=True)]
    psum x1, blocking collectives: 126 us -> 75 us  [body(): lax.psum(jnp.stack([jnp.sum(wide * first_wide), jnp.sum(wide * wide)]), (...]
    all_to_all x2 -> x0, starting transfers between devices: 21.7 us -> none  [to_rows(): lax.all_to_all(total, 'sector', split_axis=1, concat_axis=1, tiled=True)]
    all_gather x0 -> x1, blocking collectives: none -> 18.4 us  [body(): lefts = lax.all_gather(lefts, 'mpo', tiled=True)]
    reshape x0 -> x3, local copies, waits for them, and re-layouts: none -> 9.84 us  [the longest x2 5.09 us: share(): full = lax.all_gather(part, 'mpo').reshape(X, n, Z, C, n)]
  transfers between devices with their start and end apart: 4 -> 4, of which waited for: 4 -> 3; matrix products, arithmetic and copies ran while one was open for 0% -> 6% of each run, Pallas kernels for 0% -> 0%
where the time goes in v1:
time: 280 us
  waiting for transfers between devices  128 us (46%)
  blocking collectives  93.4 us (33%)
  local copies, waits for them, and re-layouts  20.8 us (7%)
  between operations  15.3 us (5%)
  matrix products  11.1 us (4%)
  other arithmetic  9.53 us (3%)
    psum x1, blocking collectives, body(): lax.psum(jnp.stack([jnp.sum(wide * first_wide), jnp.sum(wide * wide)]), (...  75 us
    all_gather x2, waiting for transfers between devices, share(): full = lax.all_gather(part, 'mpo').reshape(X, n, Z, C, n)  65.3 us
    all_gather x1, waiting for transfers between devices, body(): rights = lax.all_gather(right_here, 'sector').reshape(Z, X, C, 2, n, n)  61.9 us
    all_gather x1, blocking collectives, body(): lefts = lax.all_gather(lefts, 'mpo', tiled=True)  18.4 us
    dot_general x2, matrix products, apply_own(): jnp.einsum('btik,btkj->bij', half, rights, preferred_element_type=jnp.flo...  11.1 us
    transpose x2, local copies, waits for them, and re-layouts, share(): return full.transpose(1, 2, 0, 3, 4).reshape(n, Z * X * C, n)  7.8 us
  transfers between devices with their start and end apart: 4, of which 3 were waited for; matrix products, arithmetic and copies ran while one was open for 6% of the time, Pallas kernels for 0%

profile of v1, /device:TPU:1, one launch (start us, length us, event | category | flops | bytes accessed | tf_op | source)
XLA Modules:
  0.0 279.7 jit_solution(16110671092432052804)
XLA Ops:
  7.2 0.0 copy-start.3
  7.2 0.0 copy-start.1
  7.2 0.0 all-gather.7.cloned.1.call-start
  7.2 1.5 collective-permute-start
  8.7 0.0 collective-permute-done
  8.7 0.0 copy-start.2
  8.7 0.6 copy-done.2
  9.4 0.0 all-gather.7.cloned.1.call-update
  9.4 0.0 all-gather.11.cloned.1.call-start
  9.4 0.7 compare_bitcast_fusion.1
  10.1 0.1 gt.22
  10.2 0.8 lt.41
  11.0 0.7 iota_compare_fusion.1
  11.8 0.1 broadcast_and_fusion.1
  11.9 5.0 %and_select_fusion = bf16[128,64,128]{2,1,0:T(8,128)(2,1)S(1)} fusion(bf16[128,64,128]{2,1,0:T(8,128)(2,1)} %param.6, pred[64,128]{1,0:T(8,128)(4,1)S(1)} %iota_compare_fusion.1, pred[128,64]{1,0:T(8,128)(4,1)S(1)} %broadcast_and_fusion.1), kind=kLoop, calls=%fused_computation.6 | loop fusion | flops 2097152 | bytes 4210688 | tf_op jit(solution)/shard_map/jit(_where)/select_n | solution.py:17
  16.9 0.5 constant_dynamic-slice_fusion.1
  17.4 0.5 copy.38
  17.9 0.0 copy-done.3
  17.9 0.0 copy-done.1
  17.9 0.1 broadcast_select_fusion
  18.0 18.4 %all_gather.21 = bf16[8,128,128]{2,1,0:T(8,128)(2,1)S(1)} all-gather(bf16[2,128,128]{2,1,0:T(8,128)(2,1)S(1)} %broadcast_select_fusion), channel_id=1, replica_groups=mesh['mpo'=4,'sector'=64] {'mpo'}, dimensions={0}, use_global_device_ids=true | all-gather | bytes 327680 | tf_op jit(solution)/shard_map/all_gather | solution.py:29
  36.5 0.1 broadcast_and_fusion.2
  36.6 0.1 iota_compare_fusion
  36.7 0.9 multiply_reduce_fusion
  37.6 0.3 broadcast_and_fusion
  37.9 61.9 %all-gather.7.cloned.1.call-done = bf16[128,128,128]{2,1,0:T(8,128)(2,1)} async-done(((bf16[2,128,128]{2,1,0:T(8,128)(2,1)}), bf16[128,128,128]{2,1,0:T(8,128)(2,1)}) %all-gather.7.cloned.1.call-update) | async-done | bytes 4194320 | tf_op jit(solution)/shard_map/all_gather | solution.py:26
  99.8 4.8 %copy.23 = bf16[8,4,2,2,128,128]{5,4,3,1,2,0:T(8,128)(2,1)} copy(bf16[8,4,2,2,128,128]{5,4,3,2,1,0:T(8,128)(2,1)} %bitcast.87) | data formatting | bytes 8388608 | tf_op jit(solution)/shard_map/reshape | solution.py:26
  104.5 5.4 %fusion.29 = (f32[]{:T(128)}, bf16[128,16,128]{0,2,1:T(8,128)(2,1)S(1)}) fusion(bf16[128,8,1,2,128]{0,4,3,1,2:T(8,128)(2,1)S(1)} %copy.38, pred[128,16,128]{0,2,1:T(32,128)(4,1)S(1)} %bitcast.93, bf16[16,8,128,128]{3,2,1,0:T(8,128)(2,1)} %bitcast.88, bf16[128,16,128,1]{0,2,3,1:T(8,128)(2,1)S(1)} %bitcast.86, bf16[8,128,128]{2,1,0:T(8,128)(2,1)S(1)} %all_gather.21), kind=kOutput, calls=%fused_computation.19 | convolution fusion | flops 1077411840 | bytes 6291460 | tf_op jit(solution)/shard_map/btik,btkj->bij/dot_general | solution.py:39
  110.0 1.4 pad_maximum_fusion
  111.3 75.0 %psum.7 = f32[2]{0:T(128)S(1)} all-reduce(f32[2]{0:T(128)S(1)} %pad_maximum_fusion), channel_id=1, replica_groups=mesh['mpo'=4,'sector'=64] {'mpo','sector'}, use_global_device_ids=true, to_apply=%region_2.3 | all-reduce | flops 2 | bytes 16 | tf_op jit(solution)/shard_map/psum | solution.py:50
  186.3 0.6 fusion.36
  188.3 0.2 fusion.28
  188.5 0.0 copy-start
  188.5 5.7 %fusion.19 = bf16[128,16,128]{0,2,1:T(8,128)(2,1)} fusion(pred[128,16,128]{0,2,1:T(32,128)(4,1)S(1)} %bitcast.94, bf16[16,8,128,128]{3,2,1,0:T(8,128)(2,1)} %bitcast.89, bf16[128,16,128]{0,2,1:T(8,128)(2,1)S(1)} %fusion.28, bf16[8,128,128]{2,1,0:T(8,128)(2,1)S(1)} %all_gather.21), kind=kOutput, calls=%fused_computation.15 | convolution fusion | flops 1076363264 | bytes 5767168 | tf_op jit(solution)/shard_map/btik,btkj->bij/dot_general | solution.py:39
  194.2 0.0 all-gather.11.cloned.1.call-update
  194.2 0.0 all-gather.9.cloned.1.call-start
  194.3 0.0 copy-done
  194.3 0.7 all-gather.9.cloned.1.call-update
  195.0 31.3 %all-gather.11.cloned.1.call-done = bf16[512,16,128]{0,2,1:T(8,128)(2,1)} async-done(((bf16[128,16,128]{0,2,1:T(8,128)(2,1)}), bf16[512,16,128]{0,2,1:T(8,128)(2,1)}) %all-gather.11.cloned.1.call-update) | async-done | bytes 2097168 | tf_op jit(solution)/shard_map/all_gather | solution.py:44
  226.3 2.5 reshape.124
  228.8 3.9 %copy.29 = bf16[128,8,4,2,128]{4,3,2,1,0:T(2,128)(2,1)} copy(bf16[128,8,4,2,128]{0,2,4,3,1:T(4,128)(2,1)S(1)} %bitcast.84) | data formatting | bytes 4194304 | tf_op jit(solution)/shard_map/transpose | solution.py:45
  232.7 34.0 %all-gather.9.cloned.1.call-done = bf16[512,16,128]{0,2,1:T(8,128)(2,1)} async-done(((bf16[128,16,128]{0,2,1:T(8,128)(2,1)}), bf16[512,16,128]{0,2,1:T(8,128)(2,1)}) %all-gather.9.cloned.1.call-update) | async-done | bytes 2097168 | tf_op jit(solution)/shard_map/all_gather | solution.py:44
  266.7 2.5 reshape.122
  269.3 3.9 %copy.26 = bf16[128,8,4,2,128]{4,3,2,1,0:T(2,128)(2,1)} copy(bf16[128,8,4,2,128]{0,2,4,3,1:T(4,128)(2,1)S(1)} %bitcast.85) | data formatting | bytes 4194304 | tf_op jit(solution)/shard_map/transpose | solution.py:45
  (6 shorter events, 0.1 us)
Async XLA Ops:
  7.2 10.7 %copy-start.3 = (s32[2,1]{0,1:T(1,128)S(1)}, s32[2,1]{0,1:T(1,128)}, u32[]{:S(2)}) copy-start(s32[2,1]{0,1:T(1,128)} %param.9) | copy-start | bytes 28
  7.2 10.8 %copy-start.1 = (bf16[2,128,128]{2,1,0:T(8,128)(2,1)S(1)}, bf16[2,128,128]{2,1,0:T(8,128)(2,1)}, u32[]{:S(2)}) copy-start(bf16[2,128,128]{2,1,0:T(8,128)(2,1)} %param.7) | copy-start | bytes 196612
  7.2 92.6 %all-gather.7.cloned.1.call-start = ((), (), s32[]{:S(2)}) async-start(), calls=%async_computation | async-start | bytes 4259840 | tf_op jit(solution)/shard_map/all_gather | solution.py:26
  7.2 1.5 collective-permute-start
  8.7 0.6 copy-start.2
  9.4 216.9 %all-gather.11.cloned.1.call-start = ((), (), s32[]{:S(2)}) async-start(), calls=%async_computation.2 | async-start | bytes 2621440 | tf_op jit(solution)/shard_map/all_gather | solution.py:44
  188.5 5.8 %copy-start = (bf16[128,16,128]{0,2,1:T(8,128)(2,1)}, bf16[128,16,128]{0,2,1:T(8,128)(2,1)S(1)}, u32[]{:S(2)}) copy-start(bf16[128,16,128]{0,2,1:T(8,128)(2,1)S(1)} %fusion.28) | copy-start | bytes 1572868
  194.2 72.5 %all-gather.9.cloned.1.call-start = ((), (), s32[]{:S(2)}) async-start(), calls=%async_computation.1 | async-start | bytes 2621440 | tf_op jit(solution)/shard_map/all_gather | solution.py:44
Sparse Core Ops, SparseCore 0:
  11.4 88.3 all-gather.6
  194.3 31.8 all-gather.10
  228.6 38.0 all-gather.8

commit v2 on v1

v2 whole, which is shorter than its diff:
```python
import jax
import jax.numpy as jnp
from jax import lax
from jax.experimental import pallas as pl
from jax.experimental.pallas import tpu as pltpu
from jax.sharding import PartitionSpec as P

MESH = pl.DeviceIdType.MESH
Y, Z, X, C = 4, 8, 4, 2
N = 128
T = 8


def wrap(value, size):
    return lax.rem(value + size, size)


def images_kernel(
    v_ref, l_ref, r_ref, rows_ref, cols_ref,
    fg_ref, tot_ref,
    lcat, rbuf, xbuf, own, sums, sent, got,
    l_send, l_recv, r_send, r_recv, z_send, z_recv, c_send, c_recv,
    y_send, y_recv, f_send, o_sem, a_send, a_recv,
):
    y, s = lax.axis_index("mpo"), lax.axis_index("sector")
    z, x, c = s // (X * C), lax.rem(s // C, X), lax.rem(s, C)

    def place(y_at, z_at, x_at, c_at):
        return (y_at, (z_at * X + x_at) * C + c_at)

    def remote(src, dst, send, recv, device):
        return pltpu.make_async_remote_copy(
            src_ref=src, dst_ref=dst, send_sem=send, recv_sem=recv, device_id=device, device_id_type=MESH
        )

    here = place(y, z, x, c)
    y_near = [place(wrap(y + k, Y), z, x, c) for k in range(Y)]
    z_near = [place(y, wrap(z + k, Z), x, c) for k in range(Z)]
    x_near = [place(y, z, wrap(x + k, X), c) for k in range(X)]
    sibling = place(y, z, x, 1 - c)

    barrier = pltpu.get_barrier_semaphore()
    sources = y_near[1:] + z_near[1:] + x_near[1:] + [sibling] + [place(p, z, y, c) for p in range(Y)]
    for device in sources:
        pl.semaphore_signal(barrier, inc=1, device_id=device, device_id_type=MESH)
    pl.semaphore_wait(barrier, len(sources))

    l_copies = []
    for k in range(1, Y):
        copy = remote(l_ref, lcat.at[pl.ds(2 * y, 2)], l_send.at[k - 1], l_recv.at[k - 1], y_near[k])
        copy.start()
        l_copies.append(copy)

    def row_copy(k):
        return remote(
            r_ref, rbuf.at[z, c, pl.ds(2 * y, 2)], r_send.at[k], r_recv.at[y], place(x, z, wrap(x + k, X), c)
        )

    for k in range(1, X):
        row_copy(k).start()

    @pl.when(x == y)
    def _():
        pltpu.make_async_copy(r_ref, rbuf.at[z, c, pl.ds(2 * y, 2)], r_recv.at[y]).start()

    @pl.when(x != y)
    def _():
        row_copy(0).start()

    lcat[pl.ds(2 * y, 2)] = l_ref[...]
    for k in range(1, Y):
        from_y = wrap(y - k, Y)
        remote(l_ref, lcat.at[pl.ds(2 * from_y, 2)], l_send.at[k - 1], l_recv.at[k - 1], here).wait_recv()

    def masked(z_at, c_at):
        mask = rows_ref[...] * cols_ref[(z_at * Y + y) * C + c_at]
        return mask, v_ref[z_at, c_at].astype(jnp.float32) * mask

    def contract_left(vector):
        left = lcat[...].reshape(T * N, N)
        half = jnp.dot(left, vector, preferred_element_type=jnp.float32).astype(jnp.bfloat16)
        return half.reshape(T, N, half.shape[1])

    def beside(half):
        return jnp.concatenate([half[t] for t in range(T)], axis=1)

    def first_halves(z_at, carry):
        pair = [masked(z_at, c_at)[1].astype(jnp.bfloat16) for c_at in range(C)]
        half = contract_left(jnp.concatenate(pair, axis=1))
        for c_at in range(C):
            xbuf[z_at, c_at] = beside(half[:, :, c_at * N : (c_at + 1) * N])
        return carry

    lax.fori_loop(0, Z, first_halves, 0)
    sums[...] = jnp.zeros_like(sums)

    def images(z_at):
        def one(c_at, carry):
            mask, state = masked(z_at, c_at)
            right = rbuf[z_at, c_at].reshape(T * N, N)
            image = jnp.dot(xbuf[z_at, c_at], right, preferred_element_type=jnp.float32) * mask
            first = image.astype(jnp.bfloat16)
            own[z_at, c_at, 0] = first
            sums[0] += state * first.astype(jnp.float32)
            sums[1] += state * state
            half = beside(contract_left(first))
            image = jnp.dot(half, right, preferred_element_type=jnp.float32) * mask
            own[z_at, c_at, 1] = image.astype(jnp.bfloat16)
            return carry

        lax.fori_loop(0, C, one, 0)

    order = [z]
    for d in range(1, Z // 2):
        order += [wrap(z - d, Z), wrap(z + d, Z)]
    order.append(wrap(z + Z // 2, Z))

    def ring_copy(m, device):
        block = rbuf.at[order[m], c]
        return remote(block, block, z_send.at[m], z_recv.at[m], device)

    def hand_over(m, c_at):
        block = rbuf.at[order[m], c_at]
        return remote(block, block, c_send.at[m], c_recv.at[m], sibling)

    def send_images(m, sign):
        return remote(
            own.at[order[m]], fg_ref.at[order[m], y], y_send.at[m, sign], y_recv.at[m, sign], y_near[1 if sign == 0 else 3]
        )

    def keep_images(m):
        return pltpu.make_async_copy(own.at[order[m]], fg_ref.at[order[m], y], o_sem.at[m])

    def arrived(m, sign):
        from_y = wrap(y + (3, 1, 2)[sign], Y)
        block = fg_ref.at[order[m], from_y]
        return remote(block, block, y_send.at[m, 0], y_recv.at[m, sign], here)

    def forward(m):
        sign = m % 2
        arrived(m, sign).wait_recv()
        from_y = wrap(y + (3, 1)[sign], Y)
        block = fg_ref.at[order[m], from_y]
        remote(block, block, f_send.at[m], y_recv.at[m, 2], y_near[1 if sign == 0 else 3]).start()

    def onward(m):
        if m == 0:
            return [(0, 1, z_near[1]), (0, 2, z_near[Z - 1])]
        if m < Z - 3:
            return [(m, m + 2, z_near[1 if m % 2 else Z - 1])]
        return []

    def pass_on(m):
        for src, dst, device in onward(m):
            block = rbuf.at[order[src], c]
            remote(block, block, z_send.at[dst], z_recv.at[dst], device).start()

    def pass_last():
        source = lax.select(c == 0, wrap(z - 3, Z), wrap(z + 3, Z))
        target = place(y, lax.select(c == 0, wrap(z + 1, Z), wrap(z - 1, Z)), x, c)
        block = rbuf.at[source, c]
        return remote(block, block, z_send.at[Z - 1], z_recv.at[Z - 1], target)

    for m in range(Z):
        if m == 0:
            for p in range(Y):
                part = rbuf.at[z, c, pl.ds(2 * p, 2)]
                remote(part, part, r_send.at[0], r_recv.at[p], here).wait_recv()
        else:
            ring_copy(m, here).wait_recv()
        hand_over(m, c).start()
        pass_on(m)
        if m == Z - 2:
            pass_last().start()
        hand_over(m, 1 - c).wait_recv()
        images(order[m])
        send_images(m, 0).start()
        send_images(m, 1).start()
        keep_images(m).start()
        if m >= 2:
            forward(m - 2)

    row = lax.broadcasted_iota(jnp.int32, (8, N), 0)
    part = [jnp.sum(sums[k], axis=0, keepdims=True) for k in range(2)]
    sent[0] = jnp.where(row == 0, part[0], 0.0) + jnp.where(row == 1, part[1], 0.0)
    rounds = [(x, x_near[1:]), (z, z_near[1:]), (c, [sibling]), (y, y_near[1:])]
    base = 0
    for step, (at, devices) in enumerate(rounds):
        copies = []
        for k, device in enumerate(devices):
            copy = remote(sent.at[step], got.at[base + at], a_send.at[base + k], a_recv.at[base + k], device)
            copy.start()
            copies.append(copy)
        got[base + at] = sent[step]
        if step == 1:
            forward(Z - 2)
        if step == 3:
            forward(Z - 1)
        for copy in copies:
            copy.wait()
        total = got[base]
        for k in range(len(devices)):
            total += got[base + 1 + k]
        if step + 1 < len(rounds):
            sent[step + 1] = total
        else:
            tot_ref[...] = total
        base += len(devices) + 1

    for m in range(Z):
        arrived(m, 1 - m % 2).wait_recv()
        arrived(m, 2).wait_recv()
        keep_images(m).wait()
        send_images(m, 0).wait_send()
        send_images(m, 1).wait_send()
        remote(fg_ref.at[0, 0], fg_ref.at[0, 0], f_send.at[m], y_recv.at[m, 2], here).wait_send()
        hand_over(m, c).wait_send()
        if m > 0:
            ring_copy(m, here).wait_send()
    for copy in l_copies:
        copy.wait_send()
    for k in range(1, X):
        row_copy(k).wait_send()

    @pl.when(x != y)
    def _():
        row_copy(0).wait_send()


def images_call(v, left, right, rows, cols):
    vmem = pl.BlockSpec(memory_space=pltpu.VMEM)
    dma = pltpu.SemaphoreType.DMA
    bf16, f32 = jnp.bfloat16, jnp.float32
    rounds = X + Z + C + Y
    return pl.pallas_call(
        images_kernel,
        out_shape=(
            jax.ShapeDtypeStruct((Z, Y, C, 2, N, N), bf16),
            jax.ShapeDtypeStruct((8, N), f32),
        ),
        in_specs=[vmem] * 5,
        out_specs=(pl.BlockSpec(memory_space=pl.ANY), vmem),
        scratch_shapes=[
            pltpu.VMEM((T, N, N), bf16),
            pltpu.VMEM((Z, C, T, N, N), bf16),
            pltpu.VMEM((Z, C, N, T * N), bf16),
            pltpu.VMEM((Z, C, 2, N, N), bf16),
            pltpu.VMEM((2, N, N), f32),
            pltpu.VMEM((4, 8, N), f32),
            pltpu.VMEM((rounds, 8, N), f32),
            dma((Y - 1,)), dma((Y - 1,)),
            dma((X,)), dma((Y,)),
            dma((Z,)), dma((Z,)),
            dma((Z,)), dma((Z,)),
            dma((Z, 2)), dma((Z, 3)),
            dma((Z,)), dma((Z,)),
            dma((rounds,)), dma((rounds,)),
        ],
        compiler_params=pltpu.CompilerParams(collective_id=0, has_side_effects=True, vmem_limit_bytes=40 << 20),
    )(v, left, right, rows, cols)


def finish_kernel(tot_ref, w_ref, rows_ref, cols_ref, fg_ref, residual_ref, second_ref):
    tot = tot_ref[...]
    over = jnp.sum(tot[0:1], axis=1, keepdims=True)
    under = jnp.sum(tot[1:2], axis=1, keepdims=True)
    rayleigh = (over / under)[None]
    first = jnp.swapaxes(fg_ref[:, 0].astype(jnp.float32), 0, 1)
    image = jnp.swapaxes(fg_ref[:, 1].astype(jnp.float32), 0, 1)
    state = w_ref[...].astype(jnp.float32) * rows_ref[...] * cols_ref[...][None]
    residual_ref[...] = (first - rayleigh * state).astype(jnp.bfloat16)
    second_ref[...] = (image - rayleigh * first).astype(jnp.bfloat16)


def finish_call(tot, w, rows, cols, fg):
    step = 16
    sectors = w.shape[1]
    shape = jax.ShapeDtypeStruct(w.shape, w.dtype)
    slab = pl.BlockSpec((step, sectors, N), lambda i: (i, 0, 0))
    return pl.pallas_call(
        finish_kernel,
        grid=(N // step,),
        out_shape=(shape, shape),
        in_specs=[
            pl.BlockSpec((8, N), lambda i: (0, 0)),
            slab,
            pl.BlockSpec((step, 1, N), lambda i: (i, 0, 0)),
            pl.BlockSpec((sectors, N), lambda i: (0, 0)),
            pl.BlockSpec((sectors, 2, step, N), lambda i: (0, 0, i, 0)),
        ],
        out_specs=(slab, slab),
        compiler_params=pltpu.CompilerParams(vmem_limit_bytes=40 << 20),
    )(tot, w, rows, cols, fg)


def body(wavefunction, left_env, right_env, term_live, block_live, sector_dims):
    y, s = lax.axis_index("mpo"), lax.axis_index("sector")
    sectors = wavefunction.shape[1]
    places = jnp.arange(N, dtype=jnp.int32)
    own_dim = lax.dynamic_index_in_dim(sector_dims, s, 0, keepdims=False)
    rows = jnp.broadcast_to((places < own_dim).astype(jnp.float32)[:, None], (N, N))
    cols = ((block_live[0] > 0)[:, None] & (places[None, :] < sector_dims[:, None])).astype(jnp.float32)
    left = jnp.where((term_live > 0)[:, :, None], left_env, jnp.zeros_like(left_env))
    v = lax.dynamic_index_in_dim(wavefunction.reshape(N, Z, X, C, N), y, 2, keepdims=False)
    v = v.transpose(1, 2, 0, 3)
    fg, tot = images_call(v, left, right_env, rows, cols.reshape(sectors, 1, N))
    return finish_call(tot, wavefunction, rows.reshape(N, 1, N), cols, fg.reshape(sectors, 2, N, N))


def solution(mesh):
    return jax.shard_map(
        body,
        mesh=mesh,
        in_specs=(
            P("sector", None, None),
            P("mpo", "sector", None),
            P("mpo", "sector", None),
            P("mpo", "sector"),
            P("sector", None),
            P(),
        ),
        out_specs=(P("sector", None, None), P("sector", None, None)),
        check_vma=False,
    )
```

time: 280 us -> 81.9 us (0.29)
  waiting for transfers between devices: 128 us -> 0 us
  blocking collectives: 93.4 us -> 0 us
  Pallas kernels: 0 us -> 73.2 us
  local copies, waits for them, and re-layouts: 20.8 us -> 3.23 us
  between operations: 15.3 us -> 0.71 us
  matrix products: 11.1 us -> 0 us
  other arithmetic: 9.53 us -> 4.48 us
    all_gather x3 -> x0, waiting for transfers between devices: 127 us -> none  [the longest x2 65.3 us: share(): full = lax.all_gather(part, 'mpo').reshape(X, n, Z, C, n)]
    psum x1 -> x0, blocking collectives: 75 us -> none  [body(): lax.psum(jnp.stack([jnp.sum(wide * first_wide), jnp.sum(wide * wide)]), (...]
    pallas_call x0 -> x2, Pallas kernels: none -> 73.2 us  [the longest x1 67.5 us: images_call(): pl.pallas_call(images_kernel, out_shape=(jax.ShapeDtypeStruct((Z, Y, C, 2...]
    all_gather x1 -> x0, blocking collectives: 18.4 us -> none  [body(): lefts = lax.all_gather(lefts, 'mpo', tiled=True)]
    dot_general x2 -> x0, matrix products: 11.1 us -> none  [apply_own(): jnp.einsum('btik,btkj->bij', half, rights, preferred_element_type=jnp.flo...]
    reshape x3 -> x1, local copies, waits for them, and re-layouts: 9.84 us -> 0.19 us  [body(): rows.reshape(N, 1, N)]
    transpose x2 -> x0, local copies, waits for them, and re-layouts: 7.8 us -> none  [share(): return full.transpose(1, 2, 0, 3, 4).reshape(n, Z * X * C, n)]
    select_n x1 -> x0, other arithmetic: 4.98 us -> none  [body(): state = jnp.where(mask, wavefunction, jnp.zeros_like(wavefunction))]
  transfers between devices with their start and end apart: 4 -> 0, of which waited for: 3 -> 0; matrix products, arithmetic and copies ran while one was open for 6% -> 0% of each run, Pallas kernels for 0% -> 0%
where the time goes in v2:
time: 81.9 us; the launch traced here: 81.6 us
  Pallas kernels  73.2 us (89%)
  other arithmetic  4.48 us (5%)
  local copies, waits for them, and re-layouts  3.23 us (4%)
    pallas_call x1, Pallas kernels, images_call(): pl.pallas_call(images_kernel, out_shape=(jax.ShapeDtypeStruct((Z, Y, C, 2...  67.5 us
    pallas_call x1, Pallas kernels, finish_call(): pl.pallas_call(finish_kernel, grid=(N // step,), out_shape=(shape, shape)...  5.69 us

profile of v2, /device:TPU:1, one launch (start us, length us, event | category | flops | bytes accessed | tf_op | source)
XLA Modules:
  0.0 81.6 jit_solution(11508556720274781304)
XLA Ops:
  0.6 0.0 copy-start
  0.6 0.0 copy-start.1
  0.7 1.4 %dynamic_slice.9 = s32[1]{0:T(128)} dynamic-slice(s32[64]{0:T(128)} %param.11, s32[]{:T(128)S(6)} %select_n.14), dynamic_slice_sizes={1} | dynamic-slice | bytes 12 | tf_op jit(solution)/shard_map/jit(dynamic_index_in_dim)/dynamic_slice | solution.py:300
  2.1 0.6 compare_convert_fusion
  2.7 0.7 compare_bitcast_fusion
  3.4 0.7 compare_bitcast_fusion.1
  4.0 0.7 fusion.1.cols_ref
  4.8 0.9 %and_convert_fusion.cols_ref = f32[64,1,128]{2,1,0:T(1,128)S(1)} fusion(pred[64]{0:T(512)(128)(4,1)S(1)} %compare_bitcast_fusion, s32[64]{0:T(128)} %param.11), kind=kLoop, calls=%fused_computation.1 | loop fusion | flops 24576 | bytes 33088 | tf_op jit(solution)/shard_map/convert_element_type | solution.py:302
  5.6 0.9 %broadcast_select_fusion.l_ref = bf16[2,128,128]{2,1,0:T(8,128)(2,1)S(1)} fusion(bf16[2,128,128]{2,1,0:T(8,128)(2,1)} %param.7, pred[2]{0:T(512)(128)(4,1)S(1)} %compare_bitcast_fusion.1), kind=kLoop, calls=%fused_computation.2 | loop fusion | flops 32768 | bytes 131074 | tf_op jit(solution)/shard_map/jit(_where)/select_n | solution.py:303
  6.6 0.2 reshape.79.rows_ref
  6.8 0.1 broadcast_in_dim.26.rows_ref
  6.8 1.4 %constant_dynamic-slice_fusion = bf16[128,8,1,2,128]{4,3,2,1,0:T(2,128)(2,1)S(1)} fusion(bf16[128,8,4,2,128]{4,3,2,1,0:T(2,128)(2,1)} %bitcast.13, s32[]{:T(128)S(6)} %select_n.12), kind=kLoop, calls=%fused_computation.9 | loop fusion | bytes 1048580 | tf_op jit(solution)/shard_map/jit(dynamic_index_in_dim)/dynamic_slice | solution.py:304
  8.2 0.1 copy.11
  8.4 0.0 copy-done.1
  8.4 67.5 %shard_map.77 = (bf16[8,4,2,2,128,128]{5,4,3,2,1,0:T(8,128)(2,1)S(1)}, f32[8,128]{1,0:T(8,128)S(1)}) custom-call(bf16[8,2,128,128]{3,2,1,0:T(8,128)(2,1)S(1)} %bitcast.14, bf16[2,128,128]{2,1,0:T(8,128)(2,1)S(1)} %broadcast_select_fusion.l_ref, bf16[2,128,128]{2,1,0:T(8,128)(2,1)S(1)} %copy-done.1, f32[128,128]{1,0:T(8,128)S(1)} %broadcast_in_dim.26.rows_ref, ...), custom_call_target="tpu_custom_call" | custom-call | tf_op jit(solution)/shard_map/pallas_call | solution.py:235
  76.0 0.0 copy-done
  76.0 5.7 %shard_map.78 = (bf16[128,64,128]{2,1,0:T(8,128)(2,1)}, bf16[128,64,128]{2,1,0:T(8,128)(2,1)}) custom-call(f32[8,128]{1,0:T(8,128)S(1)} %get-tuple-element.4.tot_ref, bf16[128,64,128]{2,1,0:T(8,128)(2,1)S(1)} %copy-done, f32[128,1,128]{2,1,0:T(1,128)S(1)} %reshape.79.rows_ref, f32[64,128]{1,0:T(8,128)S(1)} %fusion.1.cols_ref, ...), custom_call_target="tpu_custom_call" | custom-call | tf_op jit(solution)/shard_map/pallas_call | solution.py:280
Async XLA Ops:
  0.6 75.3 %copy-start = (bf16[128,64,128]{2,1,0:T(8,128)(2,1)S(1)}, bf16[128,64,128]{2,1,0:T(8,128)(2,1)}, u32[]{:S(2)}) copy-start(bf16[128,64,128]{2,1,0:T(8,128)(2,1)} %w_ref.1) | copy-start | bytes 6291460
  0.6 7.8 %copy-start.1 = (bf16[2,128,128]{2,1,0:T(8,128)(2,1)S(1)}, bf16[2,128,128]{2,1,0:T(8,128)(2,1)}, u32[]{:S(2)}) copy-start(bf16[2,128,128]{2,1,0:T(8,128)(2,1)} %r_ref.1) | copy-start | bytes 196612

commit v3 on v2

v3 whole, which is shorter than its diff:
```python
import jax
import jax.numpy as jnp
from jax import lax
from jax.experimental import pallas as pl
from jax.experimental.pallas import tpu as pltpu
from jax.sharding import PartitionSpec as P

MESH = pl.DeviceIdType.MESH
Y, Z, X, C = 4, 8, 4, 2
B = Z * X * C
N = 128
PAIR = 2
T = Y * PAIR
PIECES = 2


def wrap(value, size):
    return lax.rem(value + size, size)


def images_kernel(
    live_hbm, block_hbm, dims_hbm, w_ref, l_ref, r_ref,
    fg_ref, tot_ref, rows_ref, cols_ref,
    live_ref, block_ref, dims_ref, wide, wbuf, lown, lcat, rbuf, xbuf, own, sums, sent, got,
    in_sem, l_send, l_recv, r_send, r_recv, z_send, z_recv, c_send, c_recv,
    y_send, y_recv, f_send, o_sem, a_send, a_recv,
):
    y, s = lax.axis_index("mpo"), lax.axis_index("sector")
    z, x, c = s // (X * C), lax.rem(s // C, X), lax.rem(s, C)

    def place(y_at, z_at, x_at, c_at):
        return (y_at, (z_at * X + x_at) * C + c_at)

    def remote(src, dst, send, recv, device):
        return pltpu.make_async_remote_copy(
            src_ref=src, dst_ref=dst, send_sem=send, recv_sem=recv, device_id=device, device_id_type=MESH
        )

    here = place(y, z, x, c)
    z_near = [place(y, wrap(z + k, Z), x, c) for k in range(Z)]
    y_near = [place(wrap(y + k, Y), z, x, c) for k in range(Y)]
    sibling = place(y, z, x, 1 - c)
    plane = [place(wrap(y + i, Y), z, wrap(x + j, X), c) for i in range(Y) for j in range(X)][1:]
    line = [place(y, wrap(z + i, Z), x, wrap(c + j, C)) for i in range(Z) for j in range(C)][1:]

    barrier = pltpu.get_barrier_semaphore()
    for device in plane + line:
        pl.semaphore_signal(barrier, inc=1, device_id=device, device_id_type=MESH)
    sources = (live_hbm, l_ref, block_hbm, dims_hbm, w_ref)
    targets = (live_ref, lown, block_ref, dims_ref, wbuf)
    fetch = [pltpu.make_async_copy(src, dst, in_sem.at[k]) for k, (src, dst) in enumerate(zip(sources, targets))]
    for copy in fetch:
        copy.start()
    fetch[0].wait()
    fetch[1].wait()
    for k in range(PAIR):
        lown[k] = jnp.where(live_ref[0, k] > 0, lown[k].astype(jnp.float32), 0.0).astype(jnp.bfloat16)
    lcat[pl.ds(2 * y, PAIR)] = lown[...]
    pl.semaphore_wait(barrier, len(plane) + len(line))

    def row_copy(k):
        return remote(
            r_ref, rbuf.at[z, c, pl.ds(2 * y, PAIR)], r_send.at[k], r_recv.at[y], place(x, z, wrap(x + k, X), c)
        )

    for k in range(1, X):
        row_copy(k).start()

    @pl.when(x == y)
    def _():
        pltpu.make_async_copy(r_ref, rbuf.at[z, c, pl.ds(2 * y, PAIR)], r_recv.at[y]).start()

    @pl.when(x != y)
    def _():
        row_copy(0).start()

    def left_copy(k, device):
        from_y = wrap(y - k, Y) if device is here else y
        return remote(lown, lcat.at[pl.ds(2 * from_y, PAIR)], l_send.at[k - 1], l_recv.at[k - 1], device)

    for k in range(1, Y):
        left_copy(k, y_near[k]).start()

    for copy in fetch[2:]:
        copy.wait()

    def widen(i, carry):
        chunk = wbuf[pl.ds(i * 16, 16)].astype(jnp.float32)
        wide[pl.ds(i * 16 * B, 16 * B), :] = chunk.reshape(16 * B, N)
        return carry

    lax.fori_loop(0, N // 16, widen, 0)

    rows = lax.broadcasted_iota(jnp.int32, (N, N), 0)
    lanes = lax.broadcasted_iota(jnp.int32, (N, N), 1)
    own_dim = dims_ref[s]

    def used(b):
        return jnp.where(block_ref[0, b] > 0, dims_ref[b], 0)

    def masked(z_at, c_at):
        b = (z_at * X + y) * C + c_at
        mask = (rows < own_dim) & (lanes < used(b))
        return mask, jnp.where(mask, wide[pl.ds(b, N, stride=B), :], 0.0)

    def contract_left(vector):
        left = lcat[...].reshape(T * N, N)
        half = jnp.dot(left, vector, preferred_element_type=jnp.float32).astype(jnp.bfloat16)
        return half.reshape(T, N, half.shape[1])

    def beside(half):
        return jnp.concatenate([half[t] for t in range(T)], axis=1)

    def first_halves(z_at, carry):
        pair = [masked(z_at, c_at)[1].astype(jnp.bfloat16) for c_at in range(C)]
        half = contract_left(jnp.concatenate(pair, axis=1))
        for c_at in range(C):
            xbuf[z_at, c_at] = beside(half[:, :, c_at * N : (c_at + 1) * N])
        return carry

    sums[...] = jnp.zeros_like(sums)

    def images(z_at):
        def one(c_at, carry):
            mask, state = masked(z_at, c_at)
            right = rbuf[z_at, c_at].reshape(T * N, N)
            image = jnp.dot(xbuf[z_at, c_at], right, preferred_element_type=jnp.float32)
            first = jnp.where(mask, image, 0.0).astype(jnp.bfloat16)
            own[z_at, c_at, 0] = first
            sums[0] += state * first.astype(jnp.float32)
            sums[1] += state * state
            image = jnp.dot(beside(contract_left(first)), right, preferred_element_type=jnp.float32)
            own[z_at, c_at, 1] = jnp.where(mask, image, 0.0).astype(jnp.bfloat16)
            return carry

        lax.fori_loop(0, C, one, 0)

    order = [z]
    for d in range(1, Z // 2):
        order += [wrap(z - d, Z), wrap(z + d, Z)]
    order.append(wrap(z + Z // 2, Z))
    terms = T // PIECES

    def ring_copy(z_at, m, k, device):
        block = rbuf.at[z_at, c, pl.ds(k * terms, terms)]
        return remote(block, block, z_send.at[m, k], z_recv.at[m, k], device)

    def hand_over(m, k, c_at):
        block = rbuf.at[order[m], c_at, pl.ds(k * terms, terms)]
        return remote(block, block, c_send.at[m, k], c_recv.at[m, k], sibling)

    def onward(m):
        if m == 0:
            return [(order[0], 1, z_near[1]), (order[0], 2, z_near[Z - 1])]
        if m < Z - 3:
            return [(order[m], m + 2, z_near[1 if m % 2 else Z - 1])]
        if m == Z - 2:
            source = lax.select(c == 0, order[Z - 3], order[Z - 2])
            return [(source, Z - 1, place(y, lax.select(c == 0, wrap(z + 1, Z), wrap(z - 1, Z)), x, c))]
        return []

    def ring(m, k):
        if m == 0:
            for p in range(k * terms // PAIR, (k + 1) * terms // PAIR):
                part = rbuf.at[z, c, pl.ds(PAIR * p, PAIR)]
                remote(part, part, r_send.at[0], r_recv.at[p], here).wait_recv()
        else:
            ring_copy(order[m], m, k, here).wait_recv()
        for z_at, to, device in onward(m):
            ring_copy(z_at, to, k, device).start()
        hand_over(m, k, c).start()

    def keep_images(m):
        return pltpu.make_async_copy(own.at[order[m]], fg_ref.at[order[m], y], o_sem.at[m])

    def send_images(m, way):
        return remote(
            own.at[order[m]], fg_ref.at[order[m], y], y_send.at[m, way], y_recv.at[m, way], y_near[(1, Y - 1)[way]]
        )

    def arrived(m, way):
        block = fg_ref.at[order[m], wrap(y + (3, 1, 2)[way], Y)]
        return remote(block, block, y_send.at[m, 0], y_recv.at[m, way], here)

    def forward(m, device=None):
        way = m % 2
        block = fg_ref.at[order[m], wrap(y + (3, 1)[way], Y)]
        return remote(block, block, f_send.at[m], y_recv.at[m, 2], y_near[(1, Y - 1)[way]])

    def pass_images(m):
        arrived(m, m % 2).wait_recv()
        forward(m).start()

    def compute(m):
        for k in range(PIECES):
            hand_over(m, k, 1 - c).wait_recv()
        images(order[m])
        send_images(m, 0).start()
        send_images(m, 1).start()
        keep_images(m).start()

    def sum_copy(step, k):
        at = (y * X + x, z * C + c)[step]
        return remote(
            sent.at[step], got.at[step, at], a_send.at[step, k], a_recv.at[step, k], (plane, line)[step][k]
        )

    def start_sum(step):
        for k in range(15):
            sum_copy(step, k).start()
        got[step, (y * X + x, z * C + c)[step]] = sent[step]

    def end_sum(step):
        for k in range(15):
            sum_copy(step, k).wait()
        total = got[step, 0]
        for k in range(1, 16):
            total += got[step, k]
        return total

    ring(0, 0)
    for k in range(1, Y):
        left_copy(k, here).wait_recv()
    lax.fori_loop(0, Z, first_halves, 0)
    ring(0, 1)
    compute(0)
    for d in range(1, Z // 2):
        near = (2 * d - 1, 2 * d)
        for m in near:
            ring(m, 0)
        if d == 3:
            pass_images(2)
        for m in near:
            ring(m, 1)
        for m in near:
            compute(m)
        pass_images((0, 1, 3)[d - 1])
    for k in range(PIECES):
        ring(Z - 1, k)
    compute(Z - 1)

    row = lax.broadcasted_iota(jnp.int32, (8, N), 0)
    part = [jnp.sum(sums[k], axis=0, keepdims=True) for k in range(2)]
    sent[0] = jnp.where(row == 0, part[0], 0.0) + jnp.where(row == 1, part[1], 0.0)
    start_sum(0)

    def columns(b, carry):
        cols_ref[pl.ds(b, 1), :] = jnp.where(lanes[:1] < used(b), 1.0, 0.0)
        return carry

    lax.fori_loop(0, B, columns, 0)
    rows_ref[...] = jnp.where(rows < own_dim, 1.0, 0.0)
    for m in range(Z - 4, Z - 2):
        pass_images(m)
    sent[1] = end_sum(0)
    start_sum(1)
    for m in range(Z - 2, Z):
        pass_images(m)
    tot_ref[...] = end_sum(1)

    for m in range(Z):
        arrived(m, 1 - m % 2).wait_recv()
        arrived(m, 2).wait_recv()
        keep_images(m).wait()
        send_images(m, 0).wait_send()
        send_images(m, 1).wait_send()
        forward(m).wait_send()
        for k in range(PIECES):
            hand_over(m, k, c).wait_send()
            if m > 0:
                ring_copy(order[m], m, k, here).wait_send()
    for k in range(1, Y):
        left_copy(k, here).wait_send()
    for k in range(1, X):
        row_copy(k).wait_send()

    @pl.when(x != y)
    def _():
        row_copy(0).wait_send()


def images_call(live, block, dims, w, left, right):
    vmem = pl.BlockSpec(memory_space=pltpu.VMEM)
    dma = pltpu.SemaphoreType.DMA
    bf16, f32 = jnp.bfloat16, jnp.float32
    return pl.pallas_call(
        images_kernel,
        out_shape=(
            jax.ShapeDtypeStruct((Z, Y, C, 2, N, N), bf16),
            jax.ShapeDtypeStruct((8, N), f32),
            jax.ShapeDtypeStruct((N, N), f32),
            jax.ShapeDtypeStruct((B, N), f32),
        ),
        in_specs=[pl.BlockSpec(memory_space=pltpu.HBM)] * 6,
        out_specs=(pl.BlockSpec(memory_space=pl.ANY),) + (vmem,) * 3,
        scratch_shapes=[
            pltpu.SMEM((1, PAIR), jnp.int32),
            pltpu.SMEM((1, B), jnp.int32),
            pltpu.SMEM((B,), jnp.int32),
            pltpu.VMEM((N * B, N), f32),
            pltpu.VMEM((N, B, N), bf16),
            pltpu.VMEM((PAIR, N, N), bf16),
            pltpu.VMEM((T, N, N), bf16),
            pltpu.VMEM((Z, C, T, N, N), bf16),
            pltpu.VMEM((Z, C, N, T * N), bf16),
            pltpu.VMEM((Z, C, 2, N, N), bf16),
            pltpu.VMEM((2, N, N), f32),
            pltpu.VMEM((2, 8, N), f32),
            pltpu.VMEM((2, 16, 8, N), f32),
            dma((5,)),
            dma((Y - 1,)), dma((Y - 1,)),
            dma((X,)), dma((Y,)),
            dma((Z, PIECES)), dma((Z, PIECES)),
            dma((Z, PIECES)), dma((Z, PIECES)),
            dma((Z, 2)), dma((Z, 3)),
            dma((Z,)), dma((Z,)),
            dma((2, 15)), dma((2, 15)),
        ],
        compiler_params=pltpu.CompilerParams(collective_id=0, has_side_effects=True, vmem_limit_bytes=24 << 20),
    )(live, block, dims, w, left, right)


def finish_kernel(tot_ref, rows_ref, cols_ref, w_ref, fg_ref, residual_ref, second_ref):
    tot = tot_ref[...]
    over = jnp.sum(tot[0:1], axis=1, keepdims=True)
    under = jnp.sum(tot[1:2], axis=1, keepdims=True)
    rayleigh = (over / under)[None]
    step = w_ref.shape[0]
    start = pl.multiple_of(pl.program_id(0) * step, step)
    first, image = [
        jnp.swapaxes(fg_ref[:, k, pl.ds(start, step)].astype(jnp.float32), 0, 1) for k in range(2)
    ]
    rows = rows_ref[pl.ds(start, step), :]
    state = w_ref[...].astype(jnp.float32) * cols_ref[...][None] * rows[:, None, :]
    residual_ref[...] = (first - rayleigh * state).astype(jnp.bfloat16)
    second_ref[...] = (image - rayleigh * first).astype(jnp.bfloat16)


def finish_call(tot, rows, cols, w, fg):
    step = 16
    sectors = w.shape[1]
    shape = jax.ShapeDtypeStruct(w.shape, w.dtype)
    slab = pl.BlockSpec((step, sectors, N), lambda i: (i, 0, 0))
    vmem = pl.BlockSpec(memory_space=pltpu.VMEM)
    return pl.pallas_call(
        finish_kernel,
        grid=(N // step,),
        out_shape=(shape, shape),
        in_specs=[vmem, vmem, vmem, slab, vmem],
        out_specs=(slab, slab),
        compiler_params=pltpu.CompilerParams(vmem_limit_bytes=24 << 20),
    )(tot, rows, cols, w, fg)


def body(wavefunction, left_env, right_env, term_live, block_live, sector_dims):
    arrays = (term_live.T, block_live, sector_dims, wavefunction, left_env, right_env)
    arrays = [pltpu.with_memory_space_constraint(array, pltpu.HBM) for array in arrays]
    fg, tot, rows, cols = images_call(*arrays)
    return finish_call(tot, rows, cols, wavefunction, fg.reshape(B, 2, N, N))


def solution(mesh):
    return jax.shard_map(
        body,
        mesh=mesh,
        in_specs=(
            P("sector", None, None),
            P("mpo", "sector", None),
            P("mpo", "sector", None),
            P("mpo", "sector"),
            P("sector", None),
            P(),
        ),
        out_specs=(P("sector", None, None), P("sector", None, None)),
        check_vma=False,
    )
```

time: 81.9 us -> 69.7 us (0.85)
  Pallas kernels: 73.2 us -> 68.7 us
  other arithmetic: 4.48 us -> 0 us
  local copies, waits for them, and re-layouts: 3.23 us -> 0.01 us
    pallas_call x1, Pallas kernels: 67.5 us -> 63.2 us  [images_call(): pl.pallas_call(images_kernel, out_shape=(jax.ShapeDtypeStruct((Z, Y, C, 2...]
    dynamic_slice x2 -> x0, local copies, waits for them, and re-layouts: 2.82 us -> none  [the longest x1 1.42 us: body(): lax.dynamic_index_in_dim(wavefunction.reshape(N, Z, X, C, N), y, 2, keepd...]
    convert_element_type x3 -> x0, other arithmetic: 2.24 us -> none  [the longest x2 1.59 us: body(): ((block_live[0] > 0)[:, None] & (places[None, :] < sector_dims[:, None]))...]
    select_n x1 -> x0, other arithmetic: 0.92 us -> none  [body(): jnp.where((term_live > 0)[:, :, None], left_env, jnp.zeros_like(left_env))]
where the time goes in v3:
time: 69.7 us; the launch traced here: 69.4 us
  Pallas kernels  68.7 us (99%)
    pallas_call x1, Pallas kernels, images_call(): pl.pallas_call(images_kernel, out_shape=(jax.ShapeDtypeStruct((Z, Y, C, 2...  63.2 us
    pallas_call x1, Pallas kernels, finish_call(): pl.pallas_call(finish_kernel, grid=(N // step,), out_shape=(shape, shape)...  5.47 us

profile of v3, /device:TPU:1, one launch (start us, length us, event | category | flops | bytes accessed | tf_op | source)
XLA Modules:
  0.0 69.4 jit_solution(14784159637747066505)
XLA Ops:
  0.6 0.0 copy-start
  0.6 63.2 %shard_map.77 = (bf16[8,4,2,2,128,128]{5,4,3,2,1,0:T(8,128)(2,1)S(1)}, f32[8,128]{1,0:T(8,128)S(1)}, f32[128,128]{1,0:T(8,128)S(1)}, f32[64,128]{1,0:T(8,128)S(1)}) custom-call(s32[1,2]{1,0:T(1,128)} %bitcast.3, s32[1,64]{1,0:T(1,128)} %block_hbm.1, s32[64]{0:T(128)} %dims_hbm.1, bf16[128,64,128]{2,1,0:T(8,128)(2,1)} %w_ref.3, bf16[2,128,128]{2,1,0:T(8,128)(2,1)} %l_ref.1, ...), custom_call_target="tpu_custom_call" | custom-call | tf_op jit(solution)/shard_map/pallas_call | solution.py:286
  63.9 0.0 copy-done
  63.9 5.5 %shard_map.78 = (bf16[128,64,128]{2,1,0:T(8,128)(2,1)}, bf16[128,64,128]{2,1,0:T(8,128)(2,1)}) custom-call(f32[8,128]{1,0:T(8,128)S(1)} %get-tuple-element.6.tot_ref, f32[128,128]{1,0:T(8,128)S(1)} %get-tuple-element.7.rows_ref, f32[64,128]{1,0:T(8,128)S(1)} %get-tuple-element.8.cols_ref, bf16[128,64,128]{2,1,0:T(8,128)(2,1)S(1)} %copy-done, ...), custom_call_target="tpu_custom_call" | custom-call | tf_op jit(solution)/shard_map/pallas_call | solution.py:345
Async XLA Ops:
  0.6 63.2 %copy-start = (bf16[128,64,128]{2,1,0:T(8,128)(2,1)S(1)}, bf16[128,64,128]{2,1,0:T(8,128)(2,1)}, u32[]{:S(2)}) copy-start(bf16[128,64,128]{2,1,0:T(8,128)(2,1)} %w_ref.3) | copy-start | bytes 6291460

commit v4 on v3

--- a/solution.py
+++ b/solution.py
@@ -120,20 +120,20 @@
 
     sums[...] = jnp.zeros_like(sums)
 
-    def images(z_at):
-        def one(c_at, carry):
-            mask, state = masked(z_at, c_at)
-            right = rbuf[z_at, c_at].reshape(T * N, N)
-            image = jnp.dot(xbuf[z_at, c_at], right, preferred_element_type=jnp.float32)
-            first = jnp.where(mask, image, 0.0).astype(jnp.bfloat16)
-            own[z_at, c_at, 0] = first
-            sums[0] += state * first.astype(jnp.float32)
+    def images(z_at, c_at):
+        mask, state = masked(z_at, c_at)
+        right = rbuf[z_at, c_at].reshape(T * N, N)
+        image = jnp.dot(xbuf[z_at, c_at], right, preferred_element_type=jnp.float32)
+        first = jnp.where(mask, image, 0.0).astype(jnp.bfloat16)
+        own[z_at, c_at, 0] = first
+        image = jnp.dot(beside(contract_left(first)), right, preferred_element_type=jnp.float32)
+        own[z_at, c_at, 1] = jnp.where(mask, image, 0.0).astype(jnp.bfloat16)
+
+    def add_products(z_at):
+        for c_at in range(C):
+            state = masked(z_at, c_at)[1]
+            sums[0] += state * own[z_at, c_at, 0].astype(jnp.float32)
             sums[1] += state * state
-            image = jnp.dot(beside(contract_left(first)), right, preferred_element_type=jnp.float32)
-            own[z_at, c_at, 1] = jnp.where(mask, image, 0.0).astype(jnp.bfloat16)
-            return carry
-
-        lax.fori_loop(0, C, one, 0)
 
     order = [z]
     for d in range(1, Z // 2):
@@ -159,56 +159,66 @@
             return [(source, Z - 1, place(y, lax.select(c == 0, wrap(z + 1, Z), wrap(z - 1, Z)), x, c))]
         return []
 
-    def ring(m, k):
+    def land(m, k):
         if m == 0:
             for p in range(k * terms // PAIR, (k + 1) * terms // PAIR):
                 part = rbuf.at[z, c, pl.ds(PAIR * p, PAIR)]
                 remote(part, part, r_send.at[0], r_recv.at[p], here).wait_recv()
         else:
             ring_copy(order[m], m, k, here).wait_recv()
+
+    def pass_on(m, k):
         for z_at, to, device in onward(m):
             ring_copy(z_at, to, k, device).start()
+
+    def ring(m, k):
+        land(m, k)
+        pass_on(m, k)
         hand_over(m, k, c).start()
 
     def keep_images(m):
         return pltpu.make_async_copy(own.at[order[m]], fg_ref.at[order[m], y], o_sem.at[m])
 
-    def send_images(m, way):
+    def send_images(m, c_at, way):
         return remote(
-            own.at[order[m]], fg_ref.at[order[m], y], y_send.at[m, way], y_recv.at[m, way], y_near[(1, Y - 1)[way]]
+            own.at[order[m], c_at], fg_ref.at[order[m], y, c_at],
+            y_send.at[m, c_at, way], y_recv.at[m, c_at, way], y_near[(1, Y - 1)[way]],
         )
 
-    def arrived(m, way):
-        block = fg_ref.at[order[m], wrap(y + (3, 1, 2)[way], Y)]
-        return remote(block, block, y_send.at[m, 0], y_recv.at[m, way], here)
-
-    def forward(m, device=None):
-        way = m % 2
-        block = fg_ref.at[order[m], wrap(y + (3, 1)[way], Y)]
-        return remote(block, block, f_send.at[m], y_recv.at[m, 2], y_near[(1, Y - 1)[way]])
+    def arrived(m, c_at, way):
+        block = fg_ref.at[order[m], wrap(y + (3, 1, 2)[way], Y), c_at]
+        return remote(block, block, y_send.at[m, c_at, 0], y_recv.at[m, c_at, way], here)
+
+    def forward(m, c_at):
+        way = (m + c_at) % 2
+        block = fg_ref.at[order[m], wrap(y + (3, 1)[way], Y), c_at]
+        return remote(block, block, f_send.at[m, c_at], y_recv.at[m, c_at, 2], y_near[(1, Y - 1)[way]])
 
     def pass_images(m):
-        arrived(m, m % 2).wait_recv()
-        forward(m).start()
+        for c_at in range(C):
+            arrived(m, c_at, (m + c_at) % 2).wait_recv()
+            forward(m, c_at).start()
 
     def compute(m):
         for k in range(PIECES):
             hand_over(m, k, 1 - c).wait_recv()
-        images(order[m])
-        send_images(m, 0).start()
-        send_images(m, 1).start()
+        for c_at in range(C):
+            images(order[m], c_at)
+            for way in range(2):
+                send_images(m, c_at, way).start()
         keep_images(m).start()
+        add_products(order[m])
 
     def sum_copy(step, k):
-        at = (y * X + x, z * C + c)[step]
+        at = (z * C + c, y * X + x)[step]
         return remote(
-            sent.at[step], got.at[step, at], a_send.at[step, k], a_recv.at[step, k], (plane, line)[step][k]
+            sent.at[step], got.at[step, at], a_send.at[step, k], a_recv.at[step, k], (line, plane)[step][k]
         )
 
     def start_sum(step):
         for k in range(15):
             sum_copy(step, k).start()
-        got[step, (y * X + x, z * C + c)[step]] = sent[step]
+        got[step, (z * C + c, y * X + x)[step]] = sent[step]
 
     def end_sum(step):
         for k in range(15):
@@ -219,11 +229,14 @@
         return total
 
     ring(0, 0)
+    land(0, 1)
+    hand_over(0, 1, c).start()
     for k in range(1, Y):
         left_copy(k, here).wait_recv()
-    lax.fori_loop(0, Z, first_halves, 0)
-    ring(0, 1)
+    first_halves(z, 0)
+    pass_on(0, 1)
     compute(0)
+    lax.fori_loop(1, Z, lambda k, carry: first_halves(wrap(z + k, Z), carry), 0)
     for d in range(1, Z // 2):
         near = (2 * d - 1, 2 * d)
         for m in near:
@@ -259,12 +272,13 @@
     tot_ref[...] = end_sum(1)
 
     for m in range(Z):
-        arrived(m, 1 - m % 2).wait_recv()
-        arrived(m, 2).wait_recv()
         keep_images(m).wait()
-        send_images(m, 0).wait_send()
-        send_images(m, 1).wait_send()
-        forward(m).wait_send()
+        for c_at in range(C):
+            arrived(m, c_at, 1 - (m + c_at) % 2).wait_recv()
+            arrived(m, c_at, 2).wait_recv()
+            for way in range(2):
+                send_images(m, c_at, way).wait_send()
+            forward(m, c_at).wait_send()
         for k in range(PIECES):
             hand_over(m, k, c).wait_send()
             if m > 0:
@@ -312,8 +326,8 @@
             dma((X,)), dma((Y,)),
             dma((Z, PIECES)), dma((Z, PIECES)),
             dma((Z, PIECES)), dma((Z, PIECES)),
-            dma((Z, 2)), dma((Z, 3)),
-            dma((Z,)), dma((Z,)),
+            dma((Z, C, 2)), dma((Z, C, 3)),
+            dma((Z, C)), dma((Z,)),
             dma((2, 15)), dma((2, 15)),
         ],
         compiler_params=pltpu.CompilerParams(collective_id=0, has_side_effects=True, vmem_limit_bytes=24 << 20),
@@ -337,7 +351,7 @@
 
 
 def finish_call(tot, rows, cols, w, fg):
-    step = 16
+    step = 32
     sectors = w.shape[1]
     shape = jax.ShapeDtypeStruct(w.shape, w.dtype)
     slab = pl.BlockSpec((step, sectors, N), lambda i: (i, 0, 0))

time: 69.7 us -> 67.7 us (0.971)
  Pallas kernels: 68.7 us -> 66.9 us
    pallas_call x1, Pallas kernels: 63.2 us -> 61.9 us  [images_call(): pl.pallas_call(images_kernel, out_shape=(jax.ShapeDtypeStruct((Z, Y, C, 2...]
where the time goes in v4:
time: 67.7 us; the launch traced here: 67.5 us
  Pallas kernels  66.9 us (99%)
    pallas_call x1, Pallas kernels, images_call(): pl.pallas_call(images_kernel, out_shape=(jax.ShapeDtypeStruct((Z, Y, C, 2...  61.9 us
    pallas_call x1, Pallas kernels, finish_call(): pl.pallas_call(finish_kernel, grid=(N // step,), out_shape=(shape, shape)...  5.02 us

profile of v4, /device:TPU:1, one launch (start us, length us, event | category | flops | bytes accessed | tf_op | source)
XLA Modules:
  0.0 67.5 jit_solution(7978275714543248416)
XLA Ops:
  0.6 0.0 copy-start
  0.6 61.9 %shard_map.77 = (bf16[8,4,2,2,128,128]{5,4,3,2,1,0:T(8,128)(2,1)S(1)}, f32[8,128]{1,0:T(8,128)S(1)}, f32[128,128]{1,0:T(8,128)S(1)}, f32[64,128]{1,0:T(8,128)S(1)}) custom-call(s32[1,2]{1,0:T(1,128)} %bitcast.3, s32[1,64]{1,0:T(1,128)} %block_hbm.1, s32[64]{0:T(128)} %dims_hbm.1, bf16[128,64,128]{2,1,0:T(8,128)(2,1)} %w_ref.3, bf16[2,128,128]{2,1,0:T(8,128)(2,1)} %l_ref.1, ...), custom_call_target="tpu_custom_call" | custom-call | tf_op jit(solution)/shard_map/pallas_call | solution.py:300
  62.5 0.0 copy-done
  62.5 5.0 %shard_map.78 = (bf16[128,64,128]{2,1,0:T(8,128)(2,1)}, bf16[128,64,128]{2,1,0:T(8,128)(2,1)}) custom-call(f32[8,128]{1,0:T(8,128)S(1)} %get-tuple-element.6.tot_ref, f32[128,128]{1,0:T(8,128)S(1)} %get-tuple-element.7.rows_ref, f32[64,128]{1,0:T(8,128)S(1)} %get-tuple-element.8.cols_ref, bf16[128,64,128]{2,1,0:T(8,128)(2,1)S(1)} %copy-done, ...), custom_call_target="tpu_custom_call" | custom-call | tf_op jit(solution)/shard_map/pallas_call | solution.py:359
Async XLA Ops:
  0.6 61.9 %copy-start = (bf16[128,64,128]{2,1,0:T(8,128)(2,1)S(1)}, bf16[128,64,128]{2,1,0:T(8,128)(2,1)}, u32[]{:S(2)}) copy-start(bf16[128,64,128]{2,1,0:T(8,128)(2,1)} %w_ref.3) | copy-start | bytes 6291460

commit v5 on v4

--- a/solution.py
+++ b/solution.py
@@ -247,7 +247,8 @@
             ring(m, 1)
         for m in near:
             compute(m)
-        pass_images((0, 1, 3)[d - 1])
+        if d < 3:
+            pass_images(d - 1)
     for k in range(PIECES):
         ring(Z - 1, k)
     compute(Z - 1)
@@ -263,7 +264,7 @@
 
     lax.fori_loop(0, B, columns, 0)
     rows_ref[...] = jnp.where(rows < own_dim, 1.0, 0.0)
-    for m in range(Z - 4, Z - 2):
+    for m in range(Z - 5, Z - 2):
         pass_images(m)
     sent[1] = end_sum(0)
     start_sum(1)

time: 67.7 us -> 67.7 us (level)
  no operation moved by 1% of the time
where the time goes in v5:
time: 67.7 us; the launch traced here: 67.5 us
  Pallas kernels  66.9 us (99%)
    pallas_call x1, Pallas kernels, images_call(): pl.pallas_call(images_kernel, out_shape=(jax.ShapeDtypeStruct((Z, Y, C, 2...  61.9 us
    pallas_call x1, Pallas kernels, finish_call(): pl.pallas_call(finish_kernel, grid=(N // step,), out_shape=(shape, shape)...  5.02 us

profile of v5, /device:TPU:1, one launch (start us, length us, event | category | flops | bytes accessed | tf_op | source)
XLA Modules:
  0.0 67.5 jit_solution(6331094536188310878)
XLA Ops:
  0.6 0.0 copy-start
  0.6 61.9 %shard_map.77 = (bf16[8,4,2,2,128,128]{5,4,3,2,1,0:T(8,128)(2,1)S(1)}, f32[8,128]{1,0:T(8,128)S(1)}, f32[128,128]{1,0:T(8,128)S(1)}, f32[64,128]{1,0:T(8,128)S(1)}) custom-call(s32[1,2]{1,0:T(1,128)} %bitcast.3, s32[1,64]{1,0:T(1,128)} %block_hbm.1, s32[64]{0:T(128)} %dims_hbm.1, bf16[128,64,128]{2,1,0:T(8,128)(2,1)} %w_ref.3, bf16[2,128,128]{2,1,0:T(8,128)(2,1)} %l_ref.1, ...), custom_call_target="tpu_custom_call" | custom-call | tf_op jit(solution)/shard_map/pallas_call | solution.py:301
  62.5 0.0 copy-done
  62.5 5.0 %shard_map.78 = (bf16[128,64,128]{2,1,0:T(8,128)(2,1)}, bf16[128,64,128]{2,1,0:T(8,128)(2,1)}) custom-call(f32[8,128]{1,0:T(8,128)S(1)} %get-tuple-element.6.tot_ref, f32[128,128]{1,0:T(8,128)S(1)} %get-tuple-element.7.rows_ref, f32[64,128]{1,0:T(8,128)S(1)} %get-tuple-element.8.cols_ref, bf16[128,64,128]{2,1,0:T(8,128)(2,1)S(1)} %copy-done, ...), custom_call_target="tpu_custom_call" | custom-call | tf_op jit(solution)/shard_map/pallas_call | solution.py:360
Async XLA Ops:
  0.6 61.9 %copy-start = (bf16[128,64,128]{2,1,0:T(8,128)(2,1)S(1)}, bf16[128,64,128]{2,1,0:T(8,128)(2,1)}, u32[]{:S(2)}) copy-start(bf16[128,64,128]{2,1,0:T(8,128)(2,1)} %w_ref.3) | copy-start | bytes 6291460
